TPU v7x, 32 devices: a whole 2x2x4 slice. The times are simulated.
32 devices in a mesh: dp: 2 (over x), tensor: 16 (over z, y, core).
Axes of the slice: x: 2, y: 2, z: 4, core: 2. Of those that a mesh axis runs over, the one named last changes fastest.
Arguments:
- grad_out: bfloat16 [512, 16384], P('tensor', 'dp'), may hold values from -6 to 6
- hidden: bfloat16 [512, 26624], P('dp', 'tensor'), may hold values from -0.25 to 0.25
- down_weight: bfloat16 [26624, 16384], P('tensor', 'dp'), may hold values from -0.046875 to 0.046875
Outputs:
- grad_hidden: bfloat16 [512, 26624], P('dp', 'tensor')
- grad_weight: bfloat16 [26624, 16384], P('tensor', 'dp')
All inputs are finite; a program needn't handle non-finite values.
Results may differ from a plain program's by a relative error of at most 0.0052.
Values may be sent and summed in bfloat16 or wider, within the bound.
A program may use at most 192 MiB of HBM per device.

v0:
```python
import jax
import jax.numpy as jnp
from jax import lax
from jax.sharding import PartitionSpec as P


def local(grad_out, hidden, down_weight):
    hidden_all = lax.all_gather(hidden, "dp", axis=0, tiled=True)
    grad_all = lax.all_gather(grad_out, "tensor", axis=0, tiled=True)
    weight_grad = lax.dot_general(
        hidden_all, grad_all, (((0,), (0,)), ((), ())), preferred_element_type=jnp.float32
    )
    grad_hidden = lax.psum_scatter(
        lax.dot_general(
            grad_all, down_weight, (((1,), (1,)), ((), ())), preferred_element_type=jnp.float32
        ).astype(jnp.bfloat16),
        "dp",
        scatter_dimension=0,
        tiled=True,
    )
    return (grad_hidden, weight_grad.astype(jnp.bfloat16))


def solution(mesh):
    placed = (P("tensor", "dp"), P("dp", "tensor"), P("tensor", "dp"))
    return jax.shard_map(
        local,
        mesh=mesh,
        in_specs=placed,
        out_specs=(P("dp", "tensor"), P("tensor", "dp")),
        check_vma=False,
    )
```

profile of v0, /device:TPU:0, one launch (start us, length us, event | category | flops | bytes accessed | tf_op | source)
XLA Modules:
  0.0 153.2 jit_solution(6932774043005715514)
XLA Ops:
  7.2 0.0 all-gather.3.cloned.1.call-start
  7.2 0.7 all-gather.3.cloned.1.call-update
  7.9 0.0 all-gather.5.cloned.1.call-start
  7.9 0.7 all-gather.5.cloned.1.call-update
  8.6 0.0 reduce-scatter.2.cloned.1.call-start
  8.7 79.1 %all-gather.3.cloned.1.call-done = bf16[512,8192]{1,0:T(8,128)(2,1)} async-done(((bf16[32,8192]{1,0:T(8,128)(2,1)}), bf16[512,8192]{1,0:T(8,128)(2,1)}) %all-gather.3.cloned.1.call-update) | async-done | bytes 8388624 | tf_op jit(solution)/shard_map/all_gather | solution.py:9
  87.8 22.1 %convolution_convert_fusion.1 = bf16[512,1664]{1,0:T(8,128)(2,1)} fusion(bf16[512,8192]{1,0:T(8,128)(2,1)} %all-gather.3.cloned.1.call-done, bf16[1664,8192]{1,0:T(8,128)(2,1)} %param.5), kind=kOutput, calls=%fused_computation.1 | convolution fusion | flops 13959495680 | bytes 37355520 | tf_op jit(solution)/shard_map/dot_general | solution.py:14
  109.9 0.0 reduce-scatter.2.cloned.1.call-update
  109.9 6.4 %all-gather.5.cloned.1.call-done = bf16[512,1664]{1,0:T(8,128)(2,1)} async-done(((bf16[256,1664]{1,0:T(8,128)(2,1)}), bf16[512,1664]{1,0:T(8,128)(2,1)}) %all-gather.5.cloned.1.call-update) | async-done | bytes 1703952 | tf_op jit(solution)/shard_map/all_gather | solution.py:8
  116.3 21.0 %convolution_convert_fusion = bf16[1664,8192]{1,0:T(8,128)(2,1)} fusion(bf16[512,1664]{1,0:T(8,128)(2,1)} %all-gather.5.cloned.1.call-done, bf16[512,8192]{1,0:T(8,128)(2,1)} %all-gather.3.cloned.1.call-done), kind=kOutput, calls=%fused_computation | convolution fusion | flops 13972275200 | bytes 37355520 | tf_op jit(solution)/shard_map/dot_general | solution.py:10
  137.3 9.3 %reduce-scatter.2.cloned.1.call-done = bf16[256,1664]{1,0:T(8,128)(2,1)} async-done(((bf16[512,1664]{1,0:T(8,128)(2,1)}), bf16[256,1664]{1,0:T(8,128)(2,1)}) %reduce-scatter.2.cloned.1.call-update) | async-done | bytes 851984 | tf_op jit(solution)/shard_map/reduce_scatter | solution.py:13
Async XLA Ops:
  7.2 80.6 %all-gather.3.cloned.1.call-start = ((), (), s32[]{:S(2)}) async-start(), calls=%async_computation.1 | async-start | bytes 8912896 | tf_op jit(solution)/shard_map/all_gather | solution.py:9
  7.9 108.4 %all-gather.5.cloned.1.call-start = ((), (), s32[]{:S(2)}) async-start(), calls=%async_computation.3 | async-start | bytes 2555904 | tf_op jit(solution)/shard_map/all_gather | solution.py:8
  8.6 138.0 %reduce-scatter.2.cloned.1.call-start = ((), (), s32[]{:S(2)}) async-start(), calls=%async_computation.2 | async-start | bytes 2555904 | tf_op jit(solution)/shard_map/reduce_scatter | solution.py:13
Sparse Core Ops, SparseCore 0:
  10.2 77.5 all-gather.2
  89.3 26.9 all-gather.4
  119.1 27.5 reduce-scatter.1
where the time goes:
time: 153 us
  waiting for transfers between devices  96.2 us (63%)
  matrix products  43.2 us (28%)
  between operations  13.7 us (9%)
    all_gather x1, waiting for transfers between devices, local(): grad_all = lax.all_gather(grad_out, 'tensor', axis=0, tiled=True)  79.1 us
    dot_general x1, matrix products, local(): lax.dot_general(grad_all, down_weight, (((1,), (1,)), ((), ())), preferre...  22.1 us
    dot_general x1, matrix products, local(): lax.dot_general(hidden_all, grad_all, (((0,), (0,)), ((), ())), preferred...  21 us
    reduce_scatter x1, waiting for transfers between devices, local(): lax.psum_scatter(lax.dot_general(grad_all, down_weight, (((1,), (1,)), ((...  9.33 us
    all_gather x1, waiting for transfers between devices, local(): hidden_all = lax.all_gather(hidden, 'dp', axis=0, tiled=True)  6.37 us
  transfers between devices with their start and end apart: 3, of which 3 were waited for; matrix products, arithmetic and copies ran while one was open for 28% of the time, Pallas kernels for 0%

commit v1 on v0

--- a/solution.py
+++ b/solution.py
@@ -2,11 +2,33 @@
 import jax.numpy as jnp
 from jax import lax
 from jax.sharding import PartitionSpec as P
+from jax.lax import axis_index, axis_size, ppermute
 
 
 def local(grad_out, hidden, down_weight):
     hidden_all = lax.all_gather(hidden, "dp", axis=0, tiled=True)
-    grad_all = lax.all_gather(grad_out, "tensor", axis=0, tiled=True)
+    d_next, r1, plain = (axis_size("tensor"), axis_index("tensor"), grad_out.shape[0])
+    bank = tuple((it * d_next if pp == 0 else it for pp, it in enumerate(grad_out.shape)))
+    grad_all = lax.dynamic_update_slice_in_dim(
+        jnp.zeros(bank, grad_out.dtype), grad_out, r1 * plain, axis=0
+    )
+    left_arr = after = grad_out
+    for w in range(1, d_next // 2 + 1):
+        left_arr = ppermute(
+            left_arr, "tensor", tuple(((pp, (pp + 1) % d_next) for pp in range(d_next)))
+        )
+        grad_all = lax.dynamic_update_slice_in_dim(
+            grad_all, left_arr, (r1 - w) % d_next * plain, axis=0
+        )
+        if 2 * w < d_next:
+            after = ppermute(
+                after,
+                axis_name="tensor",
+                perm=tuple(((pp, (pp - 1) % d_next) for pp in range(d_next))),
+            )
+            grad_all = lax.dynamic_update_slice_in_dim(
+                grad_all, after, (r1 + w) % d_next * plain, axis=0
+            )
     weight_grad = lax.dot_general(
         hidden_all, grad_all, (((0,), (0,)), ((), ())), preferred_element_type=jnp.float32
     )

time: 153 us -> 204 us (1.33)
  the two profiles are of different devices: /device:TPU:0 before, /device:TPU:22 now
where the time goes in v1:
time: 204 us; the launch traced here: 203 us
  waiting for transfers between devices  79.7 us (39%)
  local copies, waits for them, and re-layouts  52.6 us (26%)
  matrix products  44.3 us (22%)
  between operations  14.4 us (7%)
  starting transfers between devices  11.7 us (6%)
    ppermute x8, waiting for transfers between devices, local(): ppermute(left_arr, 'tensor', tuple(((pp, (pp + 1) % d_next) for pp in ran...  66.9 us
    unnamed x3, local copies, waits for them, and re-layouts  35 us
    dot_general x1, matrix products, local(): lax.dot_general(hidden_all, grad_all, (((0,), (0,)), ((), ())), preferred...  22.1 us
    dot_general x1, matrix products, local(): lax.dot_general(grad_all, down_weight, (((1,), (1,)), ((), ())), preferre...  22.1 us
    ppermute x7, waiting for transfers between devices, local(): ppermute(after, axis_name='tensor', perm=tuple(((pp, (pp - 1) % d_next) f...  12.6 us
    ppermute x7, starting transfers between devices, local(): ppermute(after, axis_name='tensor', perm=tuple(((pp, (pp - 1) % d_next) f...  11.1 us
    dynamic_update_slice x8, local copies, waits for them, and re-layouts, local(): lax.dynamic_update_slice_in_dim(grad_all, left_arr, (r1 - w) % d_next * p...  6.62 us
    dynamic_update_slice x7, local copies, waits for them, and re-layouts, local(): lax.dynamic_update_slice_in_dim(grad_all, after, (r1 + w) % d_next * plai...  5.78 us
  transfers between devices with their start and end apart: 17, of which 11 were waited for; matrix products, arithmetic and copies ran while one was open for 48% of the time, Pallas kernels for 0%

profile of v1, /device:TPU:22, one launch (start us, length us, event | category | flops | bytes accessed | tf_op | source)
XLA Modules:
  0.0 202.7 jit_solution(9031728398286266179)
XLA Ops:
  8.3 4.4 %broadcast_in_dim.3 = bf16[512,8192]{1,0:T(8,128)(2,1)} broadcast(bf16[]{:T(256)} %constant.89.clone.1), dimensions={} | broadcast | bytes 8388610 | tf_op jit(solution)/shard_map/broadcast_in_dim | solution.py:13
  13.5 6.4 %collective-permute-done.1 = bf16[32,8192]{1,0:T(8,128)(2,1)S(1)} collective-permute-done((bf16[32,8192]{1,0:T(8,128)(2,1)}, bf16[32,8192]{1,0:T(8,128)(2,1)S(1)}, u32[]{:S(2)}, u32[]{:S(2)}) %collective-permute-start.1) | collective-permute-done | bytes 524320 | tf_op jit(solution)/shard_map/ppermute | solution.py:24
  19.9 1.8 collective-permute-start.3
  21.7 5.7 %collective-permute-done = bf16[32,8192]{1,0:T(8,128)(2,1)S(1)} collective-permute-done((bf16[32,8192]{1,0:T(8,128)(2,1)}, bf16[32,8192]{1,0:T(8,128)(2,1)S(1)}, u32[]{:S(2)}, u32[]{:S(2)}) %collective-permute-start) | collective-permute-done | bytes 524320 | tf_op jit(solution)/shard_map/ppermute | solution.py:17
  27.4 0.8 constant_dynamic-update-slice_fusion.14
  29.0 2.9 %collective-permute-done.3 = bf16[32,8192]{1,0:T(8,128)(2,1)S(1)} collective-permute-done((bf16[32,8192]{1,0:T(8,128)(2,1)S(1)}, bf16[32,8192]{1,0:T(8,128)(2,1)S(1)}, u32[]{:S(2)}, u32[]{:S(2)}) %collective-permute-start.3) | collective-permute-done | bytes 524320 | tf_op jit(solution)/shard_map/ppermute | solution.py:24
  31.9 2.3 %collective-permute-start.5 = (bf16[32,8192]{1,0:T(8,128)(2,1)S(1)}, bf16[32,8192]{1,0:T(8,128)(2,1)S(1)}, u32[]{:S(2)}, u32[]{:S(2)}) collective-permute-start(bf16[32,8192]{1,0:T(8,128)(2,1)S(1)} %collective-permute-done.3), channel_id=1, source_target_pairs={{0,15},{1,0},{2,1},{3,2},{4,3},{5,4},{6,5},{7,6},{8,7},{9,8},{10,9... | collective-permute-start | bytes 1572872 | tf_op jit(solution)/shard_map/ppermute | solution.py:24
  34.2 13.0 %collective-permute-done.2 = bf16[32,8192]{1,0:T(8,128)(2,1)S(1)} collective-permute-done((bf16[32,8192]{1,0:T(8,128)(2,1)S(1)}, bf16[32,8192]{1,0:T(8,128)(2,1)S(1)}, u32[]{:S(2)}, u32[]{:S(2)}) %collective-permute-start.2) | collective-permute-done | bytes 524320 | tf_op jit(solution)/shard_map/ppermute | solution.py:17
  47.2 0.8 constant_dynamic-update-slice_fusion.12
  48.9 1.7 collective-permute-start.7
  50.6 10.8 %collective-permute-done.4 = bf16[32,8192]{1,0:T(8,128)(2,1)S(1)} collective-permute-done((bf16[32,8192]{1,0:T(8,128)(2,1)S(1)}, bf16[32,8192]{1,0:T(8,128)(2,1)S(1)}, u32[]{:S(2)}, u32[]{:S(2)}) %collective-permute-start.4) | collective-permute-done | bytes 524320 | tf_op jit(solution)/shard_map/ppermute | solution.py:17
  63.1 1.7 collective-permute-start.9
  64.9 10.8 %collective-permute-done.6 = bf16[32,8192]{1,0:T(8,128)(2,1)S(1)} collective-permute-done((bf16[32,8192]{1,0:T(8,128)(2,1)S(1)}, bf16[32,8192]{1,0:T(8,128)(2,1)S(1)}, u32[]{:S(2)}, u32[]{:S(2)}) %collective-permute-start.6) | collective-permute-done | bytes 524320 | tf_op jit(solution)/shard_map/ppermute | solution.py:17
  77.3 1.7 collective-permute-start.11
  79.1 10.8 %collective-permute-done.8 = bf16[32,8192]{1,0:T(8,128)(2,1)S(1)} collective-permute-done((bf16[32,8192]{1,0:T(8,128)(2,1)S(1)}, bf16[32,8192]{1,0:T(8,128)(2,1)S(1)}, u32[]{:S(2)}, u32[]{:S(2)}) %collective-permute-start.8) | collective-permute-done | bytes 524320 | tf_op jit(solution)/shard_map/ppermute | solution.py:17
  89.9 0.8 constant_dynamic-update-slice_fusion.6
  91.6 1.7 collective-permute-start.13
  93.3 5.2 %collective-permute-done.10 = bf16[32,8192]{1,0:T(8,128)(2,1)S(1)} collective-permute-done((bf16[32,8192]{1,0:T(8,128)(2,1)S(1)}, bf16[32,8192]{1,0:T(8,128)(2,1)S(1)}, u32[]{:S(2)}, u32[]{:S(2)}) %collective-permute-start.10) | collective-permute-done | bytes 524320 | tf_op jit(solution)/shard_map/ppermute | solution.py:17
  100.2 6.9 %collective-permute-done.12 = bf16[32,8192]{1,0:T(8,128)(2,1)S(1)} collective-permute-done((bf16[32,8192]{1,0:T(8,128)(2,1)S(1)}, bf16[32,8192]{1,0:T(8,128)(2,1)S(1)}, u32[]{:S(2)}, u32[]{:S(2)}) %collective-permute-start.12) | collective-permute-done | bytes 524320 | tf_op jit(solution)/shard_map/ppermute | solution.py:17
  108.0 3.3 %collective-permute-done.13 = bf16[32,8192]{1,0:T(8,128)(2,1)S(1)} collective-permute-done((bf16[32,8192]{1,0:T(8,128)(2,1)S(1)}, bf16[32,8192]{1,0:T(8,128)(2,1)S(1)}, u32[]{:S(2)}, u32[]{:S(2)}) %collective-permute-start.13) | collective-permute-done | bytes 524320 | tf_op jit(solution)/shard_map/ppermute | solution.py:24
  112.1 3.7 %collective-permute-done.14 = bf16[32,8192]{1,0:T(8,128)(2,1)S(1)} collective-permute-done((bf16[32,8192]{1,0:T(8,128)(2,1)S(1)}, bf16[32,8192]{1,0:T(8,128)(2,1)S(1)}, u32[]{:S(2)}, u32[]{:S(2)}) %collective-permute-start.14) | collective-permute-done | bytes 524320 | tf_op jit(solution)/shard_map/ppermute | solution.py:17
  116.6 22.1 %convolution_convert_fusion.1 = bf16[512,1664]{1,0:T(8,128)(2,1)} fusion(bf16[512,8192]{1,0:T(8,128)(2,1)} %constant_dynamic-update-slice_fusion, bf16[1664,8192]{1,0:T(8,128)(2,1)} %param.5), kind=kOutput, calls=%fused_computation.2 | convolution fusion | flops 13959495680 | bytes 37355520 | tf_op jit(solution)/shard_map/dot_general | solution.py:36
  138.7 22.1 %fusion = bf16[1664,8192]{0,1:T(8,128)(2,1)} fusion(bf16[512,8192]{1,0:T(8,128)(2,1)} %constant_dynamic-update-slice_fusion, bf16[512,1664]{1,0:T(8,128)(2,1)} %all-gather.2.cloned.1.call-done), kind=kOutput, calls=%fused_computation.1 | convolution fusion | flops 13972275200 | bytes 37355520 | tf_op jit(solution)/shard_map/dot_general | solution.py:32
  160.9 35.0 %copy.5 = bf16[1664,8192]{1,0:T(8,128)(2,1)} copy(bf16[1664,8192]{0,1:T(8,128)(2,1)} %fusion) | data formatting | bytes 54525952
  (34 shorter events, 11.6 us)
Async XLA Ops:
  7.2 5.5 %copy-start = (bf16[32,8192]{1,0:T(8,128)(2,1)S(1)}, bf16[32,8192]{1,0:T(8,128)(2,1)}, u32[]{:S(2)}) copy-start(bf16[32,8192]{1,0:T(8,128)(2,1)} %param.3) | copy-start | bytes 1572868
  7.2 131.5 %all-gather.2.cloned.1.call-start = ((), (), s32[]{:S(2)}) async-start(), calls=%async_computation.2 | async-start | bytes 2555904 | tf_op jit(solution)/shard_map/all_gather | solution.py:9
  7.2 12.7 %collective-permute-start.1 = (bf16[32,8192]{1,0:T(8,128)(2,1)}, bf16[32,8192]{1,0:T(8,128)(2,1)S(1)}, u32[]{:S(2)}, u32[]{:S(2)}) collective-permute-start(bf16[32,8192]{1,0:T(8,128)(2,1)} %param.3), channel_id=1, source_target_pairs={{0,15},{1,0},{2,1},{3,2},{4,3},{5,4},{6,5},{7,6},{8,7},{9,8},{10,9... | collective-permute-start | bytes 1572872 | tf_op jit(solution)/shard_map/ppermute | solution.py:24
  7.3 20.1 %collective-permute-start = (bf16[32,8192]{1,0:T(8,128)(2,1)}, bf16[32,8192]{1,0:T(8,128)(2,1)S(1)}, u32[]{:S(2)}, u32[]{:S(2)}) collective-permute-start(bf16[32,8192]{1,0:T(8,128)(2,1)} %param.3), channel_id=1, source_target_pairs={{0,1},{1,2},{2,3},{3,4},{4,5},{5,6},{6,7},{7,8},{8,9},{9,10},{10,1... | collective-permute-start | bytes 1572872 | tf_op jit(solution)/shard_map/ppermute | solution.py:17
  7.9 188.0 %reduce-scatter.2.cloned.1.call-start = ((), (), s32[]{:S(2)}) async-start(), calls=%async_computation.1 | async-start | bytes 2555904 | tf_op jit(solution)/shard_map/reduce_scatter | solution.py:35
  19.9 12.0 %collective-permute-start.3 = (bf16[32,8192]{1,0:T(8,128)(2,1)S(1)}, bf16[32,8192]{1,0:T(8,128)(2,1)S(1)}, u32[]{:S(2)}, u32[]{:S(2)}) collective-permute-start(bf16[32,8192]{1,0:T(8,128)(2,1)S(1)} %collective-permute-done.1), channel_id=1, source_target_pairs={{0,15},{1,0},{2,1},{3,2},{4,3},{5,4},{6,5},{7,6},{8,7},{9,8},{10,9... | collective-permute-start | bytes 1572872 | tf_op jit(solution)/shard_map/ppermute | solution.py:24
  27.4 19.8 %collective-permute-start.2 = (bf16[32,8192]{1,0:T(8,128)(2,1)S(1)}, bf16[32,8192]{1,0:T(8,128)(2,1)S(1)}, u32[]{:S(2)}, u32[]{:S(2)}) collective-permute-start(bf16[32,8192]{1,0:T(8,128)(2,1)S(1)} %collective-permute-done), channel_id=1, source_target_pairs={{0,1},{1,2},{2,3},{3,4},{4,5},{5,6},{6,7},{7,8},{8,9},{9,10},{10,1... | collective-permute-start | bytes 1572872 | tf_op jit(solution)/shard_map/ppermute | solution.py:17
  31.9 17.0 %collective-permute-start.5 = (bf16[32,8192]{1,0:T(8,128)(2,1)S(1)}, bf16[32,8192]{1,0:T(8,128)(2,1)S(1)}, u32[]{:S(2)}, u32[]{:S(2)}) collective-permute-start(bf16[32,8192]{1,0:T(8,128)(2,1)S(1)} %collective-permute-done.3), channel_id=1, source_target_pairs={{0,15},{1,0},{2,1},{3,2},{4,3},{5,4},{6,5},{7,6},{8,7},{9,8},{10,9... | collective-permute-start | bytes 1572872 | tf_op jit(solution)/shard_map/ppermute | solution.py:24
  47.2 14.2 %collective-permute-start.4 = (bf16[32,8192]{1,0:T(8,128)(2,1)S(1)}, bf16[32,8192]{1,0:T(8,128)(2,1)S(1)}, u32[]{:S(2)}, u32[]{:S(2)}) collective-permute-start(bf16[32,8192]{1,0:T(8,128)(2,1)S(1)} %collective-permute-done.2), channel_id=1, source_target_pairs={{0,1},{1,2},{2,3},{3,4},{4,5},{5,6},{6,7},{7,8},{8,9},{9,10},{10,1... | collective-permute-start | bytes 1572872 | tf_op jit(solution)/shard_map/ppermute | solution.py:17
  48.9 14.2 %collective-permute-start.7 = (bf16[32,8192]{1,0:T(8,128)(2,1)S(1)}, bf16[32,8192]{1,0:T(8,128)(2,1)S(1)}, u32[]{:S(2)}, u32[]{:S(2)}) collective-permute-start(bf16[32,8192]{1,0:T(8,128)(2,1)S(1)} %collective-permute-done.5), channel_id=1, source_target_pairs={{0,15},{1,0},{2,1},{3,2},{4,3},{5,4},{6,5},{7,6},{8,7},{9,8},{10,9... | collective-permute-start | bytes 1572872 | tf_op jit(solution)/shard_map/ppermute | solution.py:24
  61.5 14.2 %collective-permute-start.6 = (bf16[32,8192]{1,0:T(8,128)(2,1)S(1)}, bf16[32,8192]{1,0:T(8,128)(2,1)S(1)}, u32[]{:S(2)}, u32[]{:S(2)}) collective-permute-start(bf16[32,8192]{1,0:T(8,128)(2,1)S(1)} %collective-permute-done.4), channel_id=1, source_target_pairs={{0,1},{1,2},{2,3},{3,4},{4,5},{5,6},{6,7},{7,8},{8,9},{9,10},{10,1... | collective-permute-start | bytes 1572872 | tf_op jit(solution)/shard_map/ppermute | solution.py:17
  63.1 14.2 %collective-permute-start.9 = (bf16[32,8192]{1,0:T(8,128)(2,1)S(1)}, bf16[32,8192]{1,0:T(8,128)(2,1)S(1)}, u32[]{:S(2)}, u32[]{:S(2)}) collective-permute-start(bf16[32,8192]{1,0:T(8,128)(2,1)S(1)} %collective-permute-done.7), channel_id=1, source_target_pairs={{0,15},{1,0},{2,1},{3,2},{4,3},{5,4},{6,5},{7,6},{8,7},{9,8},{10,9... | collective-permute-start | bytes 1572872 | tf_op jit(solution)/shard_map/ppermute | solution.py:24
  75.7 14.2 %collective-permute-start.8 = (bf16[32,8192]{1,0:T(8,128)(2,1)S(1)}, bf16[32,8192]{1,0:T(8,128)(2,1)S(1)}, u32[]{:S(2)}, u32[]{:S(2)}) collective-permute-start(bf16[32,8192]{1,0:T(8,128)(2,1)S(1)} %collective-permute-done.6), channel_id=1, source_target_pairs={{0,1},{1,2},{2,3},{3,4},{4,5},{5,6},{6,7},{7,8},{8,9},{9,10},{10,1... | collective-permute-start | bytes 1572872 | tf_op jit(solution)/shard_map/ppermute | solution.py:17
  77.3 14.2 %collective-permute-start.11 = (bf16[32,8192]{1,0:T(8,128)(2,1)S(1)}, bf16[32,8192]{1,0:T(8,128)(2,1)S(1)}, u32[]{:S(2)}, u32[]{:S(2)}) collective-permute-start(bf16[32,8192]{1,0:T(8,128)(2,1)S(1)} %collective-permute-done.9), channel_id=1, source_target_pairs={{0,15},{1,0},{2,1},{3,2},{4,3},{5,4},{6,5},{7,6},{8,7},{9,8},{10,9... | collective-permute-start | bytes 1572872 | tf_op jit(solution)/shard_map/ppermute | solution.py:24
  89.9 8.6 %collective-permute-start.10 = (bf16[32,8192]{1,0:T(8,128)(2,1)S(1)}, bf16[32,8192]{1,0:T(8,128)(2,1)S(1)}, u32[]{:S(2)}, u32[]{:S(2)}) collective-permute-start(bf16[32,8192]{1,0:T(8,128)(2,1)S(1)} %collective-permute-done.8), channel_id=1, source_target_pairs={{0,1},{1,2},{2,3},{3,4},{4,5},{5,6},{6,7},{7,8},{8,9},{9,10},{10,1... | collective-permute-start | bytes 1572872 | tf_op jit(solution)/shard_map/ppermute | solution.py:17
  91.6 19.7 %collective-permute-start.13 = (bf16[32,8192]{1,0:T(8,128)(2,1)S(1)}, bf16[32,8192]{1,0:T(8,128)(2,1)S(1)}, u32[]{:S(2)}, u32[]{:S(2)}) collective-permute-start(bf16[32,8192]{1,0:T(8,128)(2,1)S(1)} %collective-permute-done.11), channel_id=1, source_target_pairs={{0,15},{1,0},{2,1},{3,2},{4,3},{5,4},{6,5},{7,6},{8,7},{9,8},{10,9... | collective-permute-start | bytes 1572872 | tf_op jit(solution)/shard_map/ppermute | solution.py:24
  98.5 8.6 %collective-permute-start.12 = (bf16[32,8192]{1,0:T(8,128)(2,1)S(1)}, bf16[32,8192]{1,0:T(8,128)(2,1)S(1)}, u32[]{:S(2)}, u32[]{:S(2)}) collective-permute-start(bf16[32,8192]{1,0:T(8,128)(2,1)S(1)} %collective-permute-done.10), channel_id=1, source_target_pairs={{0,1},{1,2},{2,3},{3,4},{4,5},{5,6},{6,7},{7,8},{8,9},{9,10},{10,1... | collective-permute-start | bytes 1572872 | tf_op jit(solution)/shard_map/ppermute | solution.py:17
  107.1 8.6 %collective-permute-start.14 = (bf16[32,8192]{1,0:T(8,128)(2,1)S(1)}, bf16[32,8192]{1,0:T(8,128)(2,1)S(1)}, u32[]{:S(2)}, u32[]{:S(2)}) collective-permute-start(bf16[32,8192]{1,0:T(8,128)(2,1)S(1)} %collective-permute-done.12), channel_id=1, source_target_pairs={{0,1},{1,2},{2,3},{3,4},{4,5},{5,6},{6,7},{7,8},{8,9},{9,10},{10,1... | collective-permute-start | bytes 1572872 | tf_op jit(solution)/shard_map/ppermute | solution.py:17
Sparse Core Ops, SparseCore 0:
  9.6 30.5 all-gather.1
  138.8 26.5 reduce-scatter.1
